TPU v7x, 128 devices: a whole 4x4x4 slice. The times are simulated.
128 devices in a mesh: pipe: 16 (over y, x_hi, core), tensor: 8 (over z, x_lo).
Axes of the slice: x: 4 (x_hi: 2, x_lo: 2; x = x_hi * 2 + x_lo), y: 4, z: 4, core: 2. Of those that a mesh axis runs over, the one named last changes fastest.
Arguments:
- forward_input: bfloat16 [16, 512, 4096], P('pipe'), may hold values from -6 to 6
- saved_input: bfloat16 [16, 512, 4096], P('pipe'), may hold values from -6 to 6
- gradient_input: bfloat16 [16, 512, 4096], P('pipe'), may hold values from -6 to 6
- roster: int32 [16, 2], P('pipe'), may hold values from 0 to 1
- sign_bits: int32 [4096], replicated, may hold values from 0 to 1
- gain: float32 [16, 2, 4096], P('pipe'), may hold values from 0.5 to 1.5
- w_query: bfloat16 [16, 2, 4096, 4096], P('pipe', None, None, 'tensor'), may hold values from -0.09375 to 0.09375
- w_key: bfloat16 [16, 2, 4096, 1024], P('pipe', None, None, 'tensor'), may hold values from -0.09375 to 0.09375
- w_value: bfloat16 [16, 2, 4096, 1024], P('pipe', None, None, 'tensor'), may hold values from -0.09375 to 0.09375
- w_out: bfloat16 [16, 2, 4096, 4096], P('pipe', None, 'tensor'), may hold values from -0.09375 to 0.09375
Outputs:
- next_activation: bfloat16 [16, 512, 4096], P('pipe')
- next_gradient: bfloat16 [16, 512, 4096], P('pipe')
All inputs are finite; a program needn't handle non-finite values.
Results may differ from a plain program's by a relative error of at most 0.015.
Values may be sent and summed in bfloat16 or wider, within the bound.
A program may use at most 192 MiB of HBM per device.

v0:
```python
import math

import jax
import jax.numpy as jnp
from jax import lax
from jax.sharding import PartitionSpec as P

HD = 128
HB = 128


eps = 1e-05


def shifted(value, axis, steps):
    count = lax.axis_size(axis)
    pairs = [(source, (source + steps) % count) for source in range(count)]
    return lax.ppermute(value, axis, pairs)


def hadamard(order):
    index = jnp.arange(order, dtype=jnp.int32)
    common = index[:, None] & index[None, :]
    parity = jnp.zeros((order, order), jnp.int32)
    for place in range(order.bit_length() - 1):
        parity = parity ^ common >> place & 1
    return (1 - 2 * parity).astype(jnp.float32)


def rotate(values, signs):
    count = values.shape[0]
    blocks = (values * signs).reshape(count, -1, HB)
    turned = jnp.einsum("rbk,kj->rbj", blocks, hadamard(HB), precision=lax.Precision.HIGHEST)
    return (turned / math.sqrt(HB)).reshape(count, -1)


def unrotate(values, signs):
    count = values.shape[0]
    blocks = values.astype(jnp.float32).reshape(count, -1, HB)
    turned = jnp.einsum("rbk,kj->rbj", blocks, hadamard(HB), precision=lax.Precision.HIGHEST)
    return (turned / math.sqrt(HB)).reshape(count, -1) * signs


def heads_part(inputs, gains, query_w, key_w, value_w, out_w):
    rows = inputs.shape[0]
    kv_count = key_w.shape[1] // HD
    q_count = query_w.shape[1] // HD
    group = q_count // kv_count
    scale = lax.rsqrt(jnp.mean(inputs * inputs, axis=-1, keepdims=True) + eps)
    normed = (inputs * scale * gains).astype(jnp.bfloat16)
    query = jnp.dot(normed, query_w, preferred_element_type=jnp.float32).astype(jnp.bfloat16)
    keys = jnp.dot(normed, key_w, preferred_element_type=jnp.float32).astype(jnp.bfloat16)
    values = jnp.dot(normed, value_w, preferred_element_type=jnp.float32).astype(jnp.bfloat16)
    query = query.reshape(rows, kv_count, group, HD).astype(jnp.float32)
    keys = keys.reshape(rows, kv_count, HD).astype(jnp.float32)
    values = values.reshape(rows, kv_count, HD).astype(jnp.float32)
    scores = jnp.einsum("qkgd,skd->kgqs", query, keys) / math.sqrt(HD)
    position = jnp.arange(rows, dtype=jnp.int32)
    allowed = position[:, None] >= position[None, :]
    scores = jnp.where(allowed, scores, -1e30)
    top = jnp.max(scores, axis=-1, keepdims=True)
    expo = jnp.exp(scores - top)
    probs = (expo / jnp.sum(expo, axis=-1, keepdims=True)).astype(jnp.bfloat16)
    context = jnp.einsum("kgqs,skd->qkgd", probs.astype(jnp.float32), values).astype(jnp.bfloat16)
    context = context.reshape(rows, q_count * HD)
    return jnp.dot(context, out_w, preferred_element_type=jnp.float32)


def pick(stack, which):
    return lax.dynamic_index_in_dim(stack[0], which, 0, keepdims=False)


def local(
    forward_input,
    saved_input,
    gradient_input,
    roster,
    sign_bits,
    gain,
    w_query,
    w_key,
    w_value,
    w_out,
):
    signs = (2 * sign_bits - 1).astype(jnp.float32)
    front = roster[0, 0]
    back = roster[0, 1]
    front_w = (pick(w_query, front), pick(w_key, front), pick(w_value, front), pick(w_out, front))
    back_w = (pick(w_query, back), pick(w_key, back), pick(w_value, back), pick(w_out, back))
    gain_front = pick(gain, front)
    gain_back = pick(gain, back)
    inputs = unrotate(forward_input[0], signs)
    grad = unrotate(gradient_input[0], signs)
    stored = saved_input[0].astype(jnp.float32)
    partial_out = heads_part(inputs, gain_front, *front_w)
    _, pull = jax.vjp(lambda v: heads_part(v, gain_back, *back_w), stored)
    partial_back = pull(grad)[0]
    mixed = lax.psum(partial_out.astype(jnp.bfloat16), "tensor").astype(jnp.float32)
    sent_activation = rotate(inputs + mixed, signs).astype(jnp.bfloat16)
    arrived = shifted(sent_activation, "pipe", 1)
    pulled = lax.psum(partial_back.astype(jnp.bfloat16), "tensor").astype(jnp.float32)
    sent_gradient = rotate(grad + pulled, signs).astype(jnp.bfloat16)
    returned = shifted(sent_gradient, "pipe", -1)
    return (arrived[None], returned[None])


def solution(mesh):
    placed = (
        P("pipe", None, None),
        P("pipe", None, None),
        P("pipe", None, None),
        P("pipe", None),
        P(),
        P("pipe", None, None),
        P("pipe", None, None, "tensor"),
        P("pipe", None, None, "tensor"),
        P("pipe", None, None, "tensor"),
        P("pipe", None, "tensor", None),
    )
    return jax.shard_map(
        local,
        mesh=mesh,
        in_specs=placed,
        out_specs=(P("pipe", None, None), P("pipe", None, None)),
        check_vma=False,
    )
```

profile of v0, /device:TPU:1, one launch (start us, length us, event | category | flops | bytes accessed | tf_op | source)
XLA Modules:
  0.0 628.2 jit_solution(7239126787473838234)
XLA Ops:
  7.2 0.0 copy-start
  7.2 0.0 all-reduce.3.cloned.1.call-start
  7.2 1.4 fusion.195
  11.2 0.1 iota_compare_fusion
  11.3 3.1 fusion.3
  15.8 3.6 fusion.96
  19.5 4.9 fusion.71
  24.4 1.3 copy.33
  25.7 0.9 copy-done.6
  26.6 1.2 copy.34
  27.9 0.0 slice-start.2
  27.9 7.8 %multiply_reduce_fusion = (f32[512]{0:T(512)S(1)}, f32[128,512,32]{1,0,2:T(8,128)S(1)}) fusion(f32[32,128]{1,0:T(8,128)S(1)} %multiply_bitcast_fusion.2, bf16[512,32,128]{2,1,0:T(8,128)(2,1)S(1)} %bitcast.297), kind=kOutput, calls=%fused_computation.27 | convolution fusion | flops 3227909632 | bytes 12601344 | tf_op jit(solution)/shard_map/rbk,kj->rbj/dot_general | solution.py:40
  35.7 0.0 slice-start.3
  35.7 4.2 bitcast_multiply_fusion.3
  39.9 3.2 fusion.65
  43.2 0.9 fusion.51
  44.0 2.0 copy-done.2
  46.0 0.9 fusion.118
  47.0 0.0 slice-start.1
  47.0 10.1 %bitcast_multiply_fusion = (bf16[512,32,128]{0,2,1:T(8,128)(2,1)S(1)}, f32[128,512,32]{1,0,2:T(8,128)}) fusion(f32[32,128]{1,0:T(8,128)S(1)} %multiply_bitcast_fusion.2, bf16[512,32,128]{2,1,0:T(8,128)(2,1)S(1)} %bitcast.294), kind=kOutput, calls=%fused_computation.17 | convolution fusion | flops 3225812992 | bytes 16793600 | tf_op jit(solution)/shard_map/rbk,kj->rbj/dot_general | solution.py:40
  57.2 3.1 fusion.68
  60.3 6.9 %convolution_convert_fusion.4 = bf16[4,512,512]{1,2,0:T(8,128)(2,1)} fusion(bf16[128,4,512]{2,0,1:T(8,128)(2,1)} %bitcast.317, bf16[1,2,4096,128]{3,2,1,0:T(8,128)(2,1)} %param.18, s32[]{:T(128)S(6)} %select_n.32, bf16[1,512,4096]{2,1,0:T(8,128)(2,1)} %param.11, f32[4096]{0:T(1024)S(1)} %bitcast.309, f32[512]{0:T(512)S(1)} %fusion.149), kind=kOutput, calls=%fused_computation.89 | convolution fusion | flops 814809088 | bytes 7882756 | tf_op jit(solution)/shard_map/transpose(jvp(kgqs,skd->qkgd))/dot_general | solution.py:64
  67.2 8.8 %convert_reduce_fusion = (f32[4,512]{1,0:T(4,128)S(1)}, pred[1,4,512,512]{2,3,1,0:T(32,128)(4,1)}, f32[4,512]{1,0:T(4,128)S(1)}, f32[4,512]{1,0:T(4,128)S(1)}, f32[512,512,4]{1,0,2:T(8,128)}) fusion(f32[4,512]{1,0:T(4,128)S(1)} %get-tuple-element.20, f32[512,512,4]{1,0,2:T(8,128)} %copy-done.2, pred[512,512]{0,1:T(8,128)(4,1)S(1)} %iota_compare_fusion, ...), kind=kOutput, calls=%fused_computation.62 | convolution fusion | flops 818997248 | bytes 17604612 | tf_op jit(solution)/shard_map/qkgd,skd->kgqs/dot_general | solution.py:57
  76.0 5.4 fusion.189
  81.4 0.5 copy-done.8
  81.9 0.2 copy-done.14
  82.1 3.5 fusion.74
  85.6 9.2 %convolution_convert_fusion = bf16[512,4096]{1,0:T(8,128)(2,1)} fusion(bf16[512,4,128]{0,2,1:T(8,128)(2,1)S(1)} %bitcast.306, pred[1,4,512,512]{2,3,1,0:T(32,128)(4,1)} %get-tuple-element.9, f32[4,512]{1,0:T(4,128)S(1)} %negate_divide_fusion, pred[512,512]{0,1:T(8,128)(4,1)S(1)} %iota_compare_fusion, bf16[1,2,4096,128]{3,2,1,0:T(8,128)(2,1)S(1)} %copy-done, ...), kind=kOutput, calls=%fused_computation.28 | convolution fusion | flops 819003392 | bytes 13402116 | tf_op jit(solution)/shard_map/transpose(jvp())/dot_general | solution.py:52
  94.8 5.8 fusion.77
  100.7 6.6 %convolution_convert_fusion.3 = bf16[512,4096]{1,0:T(8,128)(2,1)} fusion(bf16[512,512]{0,1:T(8,128)(2,1)S(1)} %bitcast.321, bf16[1,2,512,4096]{3,2,1,0:T(8,128)(2,1)} %param.19, s32[]{:T(128)S(6)} %select_n.30), kind=kOutput, calls=%fused_computation.31 | convolution fusion | flops 2149580800 | bytes 8912900 | tf_op jit(solution)/shard_map/dot_general | solution.py:66
  107.3 6.8 %convolution_convert_fusion.2 = bf16[512,4096]{1,0:T(8,128)(2,1)} fusion(bf16[512,512]{0,1:T(8,128)(2,1)S(1)} %bitcast.320, bf16[1,2,4096,512]{3,2,1,0:T(8,128)(2,1)} %param.16, s32[]{:T(128)S(6)} %select_n.32), kind=kOutput, calls=%fused_computation.30 | convolution fusion | flops 2149580800 | bytes 8912900 | tf_op jit(solution)/shard_map/transpose(jvp())/dot_general | solution.py:51
  114.1 11.8 %fusion.4 = (f32[512]{0:T(512)S(1)}, bf16[512,4096]{1,0:T(8,128)(2,1)}) fusion(bf16[1,512,4096]{2,1,0:T(8,128)(2,1)} %param.11, f32[4096]{0:T(1024)S(1)} %bitcast.310, bf16[512,4096]{1,0:T(8,128)(2,1)} %convolution_convert_fusion.2, bf16[512,4096]{1,0:T(8,128)(2,1)} %convolution_convert_fusion, bf16[1,2,4096,128]{3,2,1,0:T(8,128)(2,1)S(1)} %copy-done.11, ...), kind=kOutput, calls=%fused_computation.7 | convolution fusion | flops 835780096 | bytes 22841348 | tf_op jit(solution)/shard_map/transpose(jvp())/dot_general | solution.py:53
  125.9 6.1 fusion.7
  132.0 0.0 all-reduce.3.cloned.1.call-update
  132.0 9.0 %copy.13 = f32[512,4096]{1,0:T(8,128)} copy(f32[512,4096]{0,1:T(8,128)} %bitcast.292) | data formatting | bytes 16777216 | tf_op jit(solution)/shard_map/reshape | solution.py:41
  141.0 8.3 %bitcast_multiply_fusion.1 = f32[512,32,128]{0,2,1:T(8,128)} fusion(f32[128,512,32]{1,0,2:T(8,128)} %get-tuple-element.25), kind=kLoop, calls=%fused_computation.18 | loop fusion | flops 2097152 | bytes 16777216 | tf_op jit(solution)/shard_map/div | solution.py:41
  149.3 9.0 %copy.19 = f32[512,4096]{1,0:T(8,128)} copy(f32[512,4096]{0,1:T(8,128)} %bitcast.293) | data formatting | bytes 16777216 | tf_op jit(solution)/shard_map/reshape | solution.py:41
  158.2 317.3 %all-reduce.3.cloned.1.call-done = (bf16[512,4096]{1,0:T(8,128)(2,1)}, bf16[512,4096]{1,0:T(8,128)(2,1)}) async-done(((bf16[512,4096]{1,0:T(8,128)(2,1)}, bf16[512,4096]{1,0:T(8,128)(2,1)}), (bf16[512,4096]{1,0:T(8,128)(2,1)}, bf16[512,4096]{1,0:T(8,128)(2,1)})) %all-reduce.3.cloned.1.call-update) | async-done | bytes 8388624 | tf_op jit(solution)/shard_map/psum | solution.py:98
  475.6 13.6 %multiply_bitcast_fusion = (f32[64,32,8,128]{3,2,1,0:T(8,128)}, f32[64,32,8,128]{3,2,1,0:T(8,128)S(1)}) fusion(bf16[512,4096]{1,0:T(8,128)(2,1)} %get-tuple-element.7, f32[512,4096]{1,0:T(8,128)} %copy.19, f32[4096]{0:T(1024)S(1)} %add_convert_fusion, bf16[512,4096]{1,0:T(8,128)(2,1)} %get-tuple-element.6, f32[512,4096]{1,0:T(8,128)} %copy.13), kind=kLoop, calls=%fused_computation.22 | loop fusion | flops 16777216 | bytes 41959424
  489.2 13.2 %multiply_convert_fusion = bf16[512,32,128]{0,2,1:T(8,128)(2,1)} fusion(f32[64,32,8,128]{3,2,1,0:T(8,128)} %get-tuple-element.16), kind=kOutput, calls=%fused_computation.21 | convolution fusion | flops 3225812992 | bytes 12582912 | tf_op jit(solution)/shard_map/rbk,kj->rbj/dot_general | solution.py:33
  502.4 9.7 %multiply_convert_fusion.1 = bf16[512,32,128]{0,2,1:T(8,128)(2,1)} fusion(f32[64,32,8,128]{3,2,1,0:T(8,128)S(1)} %get-tuple-element.17), kind=kOutput, calls=%fused_computation.24 | convolution fusion | flops 3225812992 | bytes 12582912 | tf_op jit(solution)/shard_map/rbk,kj->rbj/dot_general | solution.py:33
  512.2 6.3 %copy.17 = bf16[512,4096]{1,0:T(8,128)(2,1)} copy(bf16[512,4096]{0,1:T(8,128)(2,1)} %bitcast.296) | data formatting | bytes 8388608 | tf_op jit(solution)/shard_map/convert_element_type | solution.py:99
  518.5 3.0 collective-permute-start
  521.5 6.3 %copy.24 = bf16[512,4096]{1,0:T(8,128)(2,1)} copy(bf16[512,4096]{0,1:T(8,128)(2,1)} %bitcast.295) | data formatting | bytes 8388608 | tf_op jit(solution)/shard_map/convert_element_type | solution.py:102
  527.8 74.7 %collective-permute-done = bf16[512,4096]{1,0:T(8,128)(2,1)} collective-permute-done((bf16[512,4096]{1,0:T(8,128)(2,1)}, bf16[512,4096]{1,0:T(8,128)(2,1)}, u32[]{:S(2)}, u32[]{:S(2)}) %collective-permute-start) | collective-permute-done | bytes 4194336 | tf_op jit(solution)/shard_map/ppermute | solution.py:18
  602.5 11.5 %collective-permute-done.1 = bf16[512,4096]{1,0:T(8,128)(2,1)S(1)} collective-permute-done((bf16[512,4096]{1,0:T(8,128)(2,1)}, bf16[512,4096]{1,0:T(8,128)(2,1)S(1)}, u32[]{:S(2)}, u32[]{:S(2)}) %collective-permute-start.1) | collective-permute-done | bytes 4194336 | tf_op jit(solution)/shard_map/ppermute | solution.py:18
  614.0 4.8 copy.62
  618.9 2.0 copy.63
  (42 shorter events, 0.2 us)
Async XLA Ops:
  7.2 8.6 %copy-start = (bf16[1,2,4096,128]{3,2,1,0:T(8,128)(2,1)S(1)}, bf16[1,2,4096,128]{3,2,1,0:T(8,128)(2,1)}, u32[]{:S(2)}) copy-start(bf16[1,2,4096,128]{3,2,1,0:T(8,128)(2,1)} %param.17) | copy-start | bytes 6291460
  7.2 7.2 %copy-start.9 = (s32[4096]{0:T(1024)S(1)}, s32[4096]{0:T(1024)}, u32[]{:S(2)}) copy-start(s32[4096]{0:T(1024)} %param.14) | copy-start | bytes 49156
  7.2 8.5 %copy-start.10 = (f32[1,2,4096]{2,1,0:T(2,128)S(1)}, f32[1,2,4096]{2,1,0:T(2,128)}, u32[]{:S(2)}) copy-start(f32[1,2,4096]{2,1,0:T(2,128)} %param.15) | copy-start | bytes 98308
  7.2 468.4 %all-reduce.3.cloned.1.call-start = ((), (), s32[]{:S(2)}) async-start(), calls=%async_computation | async-start | bytes 16777216 | tf_op jit(solution)/shard_map/psum | solution.py:98
  15.8 3.7 copy-start.4
  19.5 4.9 copy-start.5
  24.4 2.2 copy-start.6
  27.9 12.1 %slice-start.2 = ((s8[8388608]{0:T(1024)(128)(4,1)}), s8[4194304]{0:T(1024)(128)(4,1)S(1)}, s32[]{:S(2)}) async-start(s8[8388608]{0:T(1024)(128)(4,1)} %bitcast.315), calls=%async_computation.3 | async-start | bytes 8388608
  35.7 4.2 slice-start.3
  39.9 3.2 copy-start.7
  44.0 2.0 copy-start.2
  46.0 11.1 %slice-start = ((s8[8388608]{0:T(1024)(128)(4,1)}), s8[4194304]{0:T(1024)(128)(4,1)S(1)}, s32[]{:S(2)}) async-start(s8[8388608]{0:T(1024)(128)(4,1)} %bitcast.313), calls=%async_computation.1 | async-start | bytes 8388608
  47.0 10.2 %slice-start.1 = ((s8[8388608]{0:T(1024)(128)(4,1)}), s8[4194304]{0:T(1024)(128)(4,1)S(1)}, s32[]{:S(2)}) async-start(s8[8388608]{0:T(1024)(128)(4,1)} %bitcast.313), calls=%async_computation.2 | async-start | bytes 8388608
  76.0 5.4 copy-start.3
  76.0 5.9 copy-start.8
  76.0 6.1 copy-start.14
  100.7 6.6 %copy-start.13 = (bf16[512,4,128]{0,2,1:T(8,128)(2,1)S(1)}, bf16[512,4,128]{0,2,1:T(8,128)(2,1)}, u32[]{:S(2)}) copy-start(bf16[512,4,128]{0,2,1:T(8,128)(2,1)} %fusion.74) | copy-start | bytes 1572868
  107.3 6.8 %copy-start.11 = (bf16[1,2,4096,128]{3,2,1,0:T(8,128)(2,1)S(1)}, bf16[1,2,4096,128]{3,2,1,0:T(8,128)(2,1)}, u32[]{:S(2)}) copy-start(bf16[1,2,4096,128]{3,2,1,0:T(8,128)(2,1)} %param.18) | copy-start | bytes 6291460
  107.3 6.8 %copy-start.12 = (bf16[512,512]{0,1:T(8,128)(2,1)S(1)}, bf16[512,512]{0,1:T(8,128)(2,1)}, u32[]{:S(2)}) copy-start(bf16[512,512]{0,1:T(8,128)(2,1)} %fusion.68) | copy-start | bytes 1572868
  518.5 84.1 %collective-permute-start = (bf16[512,4096]{1,0:T(8,128)(2,1)}, bf16[512,4096]{1,0:T(8,128)(2,1)}, u32[]{:S(2)}, u32[]{:S(2)}) collective-permute-start(bf16[512,4096]{1,0:T(8,128)(2,1)} %copy.17), channel_id=1, source_target_pairs={{0,8},{8,16},{16,24},{24,32},{32,40},{40,48},{48,56},{56,64},{64,7... | collective-permute-start | bytes 12582920 | tf_op jit(solution)/shard_map/ppermute | solution.py:18
  527.8 86.2 %collective-permute-start.1 = (bf16[512,4096]{1,0:T(8,128)(2,1)}, bf16[512,4096]{1,0:T(8,128)(2,1)S(1)}, u32[]{:S(2)}, u32[]{:S(2)}) collective-permute-start(bf16[512,4096]{1,0:T(8,128)(2,1)} %copy.24), channel_id=1, source_target_pairs={{0,120},{8,0},{16,8},{24,16},{32,24},{40,32},{48,40},{56,48},{64,5... | collective-permute-start | bytes 12582920 | tf_op jit(solution)/shard_map/ppermute | solution.py:18
  614.0 6.9 %copy-start.1 = (bf16[1,2,4096,128]{3,2,1,0:T(8,128)(2,1)S(1)}, bf16[1,2,4096,128]{3,2,1,0:T(8,128)(2,1)}, u32[]{:S(2)}) copy-start(bf16[1,2,4096,128]{3,2,1,0:T(8,128)(2,1)} %param.17) | copy-start | bytes 6291460
Sparse Core Ops, SparseCore 0:
  132.1 343.3 all-reduce.2
where the time goes:
time: 638 us; the launch traced here: 628 us
  waiting for transfers between devices  404 us (63%)
  matrix products  116 us (18%)
  local copies, waits for them, and re-layouts  45.1 us (7%)
  other arithmetic  41.7 us (7%)
  between operations  18.7 us (3%)
    psum x1, waiting for transfers between devices, local(): lax.psum(partial_out.astype(jnp.bfloat16), 'tensor').astype(jnp.float32)  317 us
    ppermute x2, waiting for transfers between devices, shifted(): return lax.ppermute(value, axis, pairs)  86.2 us
    dot_general x2, matrix products, rotate(): jnp.einsum('rbk,kj->rbj', blocks, hadamard(HB), precision=lax.Precision.H...  23 us
    dot_general x2, matrix products, unrotate(): jnp.einsum('rbk,kj->rbj', blocks, hadamard(HB), precision=lax.Precision.H...  18 us
    reshape x2, local copies, waits for them, and re-layouts, unrotate(): return (turned / math.sqrt(HB)).reshape(count, -1) * signs  17.9 us
    dot_general x3, matrix products, heads_part(): jnp.dot(normed, query_w, preferred_element_type=jnp.float32)  14.9 us
    unnamed x3, other arithmetic  13.6 us
    dot_general x3, matrix products, heads_part(): scores = jnp.einsum('qkgd,skd->kgqs', query, keys) / math.sqrt(HD)  13.1 us
  transfers between devices with their start and end apart: 3, of which 3 were waited for; matrix products, arithmetic and copies ran while one was open for 5% of the time, Pallas kernels for 0%

commit v1 on v0

v1 whole, which is shorter than its diff:
```python
import functools
import math

import jax
import jax.numpy as jnp
from jax import lax
from jax.experimental import pallas as pl
from jax.experimental.pallas import tpu as pltpu
from jax.sharding import PartitionSpec as P

MESH = pl.DeviceIdType.MESH
D = 4096
ROWS = 512
HD = 128
HB = 128
HEADS = 4
BLOCK = 64
CA = 2304
CB = D - CA
HALF = CB // 2
TILE = 256
EPS = 1e-05
UNIT = 1.0 / math.sqrt(HB)
SM = 1.0 / math.sqrt(HD)
A = pl.ds(0, CA)
B = pl.ds(CA, CB)
BL = pl.ds(CA, HALF)
BR = pl.ds(CA + HALF, HALF)
F32 = jnp.float32
BF16 = jnp.bfloat16


def dot(a, b):
    return jnp.dot(a, b, preferred_element_type=F32)


def dot_nt(a, b):
    return lax.dot_general(a, b, (((1,), (1,)), ((), ())), preferred_element_type=F32)


def dot_tn(a, b):
    return lax.dot_general(a, b, (((0,), (0,)), ((), ())), preferred_element_type=F32)


def tile(c, width=TILE):
    return pl.ds(pl.multiple_of(c * width, width), width)


def loop(count, body):
    lax.fori_loop(0, count, lambda i, _: (body(i), 0)[1], 0)


def hadamard_pair():
    i = lax.broadcasted_iota(jnp.int32, (2 * HB, 2 * HB), 0)
    j = lax.broadcasted_iota(jnp.int32, (2 * HB, 2 * HB), 1)
    c = i & j & (HB - 1)
    c = c ^ (c >> 4)
    c = c ^ (c >> 2)
    c = c ^ (c >> 1)
    value = (1 - 2 * (c & 1)).astype(F32)
    return jnp.where((i >> 7) == (j >> 7), value, 0.0).astype(BF16)


def kernel(
    roster, bits, gain, fin, sav, gin, wq, wk, wv, wo,
    of, ob,
    fv, sv, gv, wqv, wkv, wov, fr, sr, gr,
    had, rows_scale, qv, kvv, ctx, dctx, dq, dkv, dkvb,
    ra_f, rbx_f, rbz_f, ra_b, rbx_b, rbz_b, total, stage_f, stage_b,
    load, send, recv,
):
    p = lax.axis_index("pipe")
    t = lax.axis_index("tensor")
    x = lax.rem(t, 2)
    z = lax.div(t, 2)
    n_pipe = lax.axis_size("pipe")
    zp, z2, zm = lax.rem(z + 1, 4), lax.rem(z + 2, 4), lax.rem(z + 3, 4)
    par = lax.rem(p, 2)
    swap = 1 - 2 * x
    up, down, side = (p, zp * 2 + x), (p, zm * 2 + x), (p, t + swap)
    after = (lax.rem(p + 1, n_pipe), t + par * swap)
    before = (lax.rem(p + n_pipe - 1, n_pipe), t + (1 - par) * swap)
    held_f = t + (1 - par) * swap
    held_b = t + par * swap

    def block(index):
        return pl.ds(pl.multiple_of(index * BLOCK, BLOCK), BLOCK)

    mine = block(t)
    loads = [
        (fin, fv), (wk, wkv.at[:, :, pl.ds(0, HD)]), (wv, wkv.at[:, :, pl.ds(HD, HD)]), (wq, wqv), (wo, wov),
        (sav, sv), (gin, gv), (fin.at[mine], fr), (sav.at[mine], sr), (gin.at[mine], gr),
    ]
    loads = [pltpu.make_async_copy(a, b, load.at[i]) for i, (a, b) in enumerate(loads)]
    for one in loads:
        one.start()
    l_fin, l_wk, l_wv, l_wq, l_wo, l_sav, l_gin, l_fr, l_sr, l_gr = loads

    barrier = pltpu.get_barrier_semaphore()
    for other in (up, down, side, after, before):
        pl.semaphore_signal(barrier, inc=1, device_id=other, device_id_type=MESH)

    front, back = roster[0], roster[1]
    had[...] = hadamard_pair()

    def signs(cols):
        return (2 * bits[:, cols] - 1).astype(F32)

    counter = [0]
    started = []

    def push(src, dst, device):
        i = counter[0]
        counter[0] += 1
        copy = pltpu.make_async_remote_copy(
            src_ref=src, dst_ref=dst, send_sem=send.at[i], recv_sem=recv.at[i], device_id=device, device_id_type=MESH
        )
        copy.start()
        started.append(copy)
        return copy

    def scales(ref):
        def body(i):
            rows = tile(i, 32)
            v = ref[rows, :].astype(F32)
            s = lax.rsqrt(jnp.sum(v * v, axis=-1, keepdims=True) * (1.0 / D) + EPS)
            rows_scale[rows, :] = jnp.broadcast_to(s, (32, 128))
        loop(ROWS // 32, body)

    def project(ref, which):
        kvv[...] = dot(ref[...], wkv[which]).astype(BF16)
        def body(n):
            cols = tile(n)
            qv[:, cols] = dot(ref[...], wqv[which, :, cols]).astype(BF16)
        return body

    def probabilities(q, lo, size):
        n = lo + size
        s = dot_nt(q, kvv[pl.ds(0, n), pl.ds(0, HD)]) * SM
        row = lax.broadcasted_iota(jnp.int32, (size, n), 0) + lo
        col = lax.broadcasted_iota(jnp.int32, (size, n), 1)
        s = jnp.where(row >= col, s, -1e30)
        e = jnp.exp(s - jnp.max(s, axis=-1, keepdims=True))
        return e / jnp.sum(e, axis=-1, keepdims=True)

    def add(ref, base, cols, *terms):
        def body(i):
            rows = pl.ds(pl.multiple_of(base * BLOCK + i * 16, 16), 16)
            value = ref[rows, cols].astype(F32)
            for term in terms:
                value += term[pl.ds(pl.multiple_of(i * 16, 16), 16), :].astype(F32)
            ref[rows, cols] = value.astype(BF16)
        loop(BLOCK // 16, body)

    def scatter(part, ra, rbx, rbz, whole):
        c = {}

        def first_a():
            c["m0"] = push(part.at[block(2 * z2), A], ra.at[0], up)
            c["p0"] = push(part.at[block(2 * z2 + 1), A], ra.at[1], down)
            c["m1"] = push(part.at[block(2 * zp + 1), A], ra.at[2], up)
            c["p1"] = push(part.at[block(2 * zm), A], ra.at[3], down)

        def first_b():
            for k, zz in ((2, z2), (1, zp), (3, zm), (0, z)):
                c["x", k] = push(part.at[block(2 * zz + 1 - x), B], rbx.at[k], side)

        def s1():
            c["m0"].wait_recv()
            add(part, 2 * zp, A, ra.at[0])
            c["m2"] = push(part.at[block(2 * zp), A], ra.at[4], up)
            c["p0"].wait_recv()
            add(part, 2 * zm + 1, A, ra.at[1])
            c["p2"] = push(part.at[block(2 * zm + 1), A], ra.at[5], down)
            c["x", 2].wait_recv()
            add(part, 2 * z2 + x, B, rbx.at[2])
            c["bm0"] = push(part.at[block(2 * z2 + x), BL], rbz.at[0], up)
            c["bp0"] = push(part.at[block(2 * z2 + x), BR], rbz.at[1], down)

        def s2():
            c["x", 1].wait_recv()
            add(part, 2 * zp + x, B, rbx.at[1])
            c["bm1"] = push(part.at[block(2 * zp + x), BR], rbz.at[2], up)
            c["x", 3].wait_recv()
            add(part, 2 * zm + x, B, rbx.at[3])
            c["bp1"] = push(part.at[block(2 * zm + x), BL], rbz.at[3], down)
            c["bm0"].wait_recv()
            add(part, 2 * zp + x, BL, rbz.at[0])
            c["bm2"] = push(part.at[block(2 * zp + x), BL], rbz.at[4], up)
            c["bp0"].wait_recv()
            add(part, 2 * zm + x, BR, rbz.at[1])
            c["bp2"] = push(part.at[block(2 * zm + x), BR], rbz.at[5], down)

        def s3():
            for name in ("m1", "m2", "p1", "p2"):
                c[name].wait_recv()
            add(part, 2 * z + 1 - x, A, ra.at[2 + 2 * x], ra.at[5 - 2 * x])
            c["ax"] = push(part.at[block(2 * z + 1 - x), A], ra.at[6], side)

        def s4():
            for name in ("ax", ("x", 0), "bm1", "bm2", "bp1", "bp2"):
                c[name].wait_recv()

            def body(i):
                rows = tile(i, 16)
                own = pl.ds(pl.multiple_of(t * BLOCK + i * 16, 16), 16)
                get = lambda ref, *at: ref[at].astype(F32)
                whole[rows, A] = (
                    get(part, own, A) + get(ra, 4 - 2 * x, rows) + get(ra, 3 + 2 * x, rows) + get(ra, 6, rows)
                )
                whole[rows, BL] = (
                    get(part, own, BL) + get(rbx, 0, rows, pl.ds(0, HALF)) + get(rbz, 4, rows) + get(rbz, 3, rows)
                )
                whole[rows, BR] = (
                    get(part, own, BR) + get(rbx, 0, rows, pl.ds(HALF, HALF)) + get(rbz, 2, rows) + get(rbz, 5, rows)
                )
            loop(BLOCK // 16, body)

        return first_a, first_b, s1, s2, s3, s4

    def turn(whole, held, stage):
        def body(n):
            cols = tile(n)
            v = whole[:, cols] * signs(cols)
            hi = v.astype(BF16)
            lo = (v - hi.astype(F32)).astype(BF16)
            y = dot(hi, had[...]) + dot(lo, had[...])
            stage[:, cols] = (held[:, cols].astype(F32) + y * UNIT).astype(BF16)
        loop(D // TILE, body)

    def gather(out, stage, device, r):
        c = {}
        rx = lax.rem(r, 2)

        def go(zz, xx, cols, device):
            here = out.at[block(2 * zz + xx), cols]
            return push(here, here, device)

        def shift():
            c["s"] = push(stage, out.at[mine], device)

        def g1():
            c["s"].wait_recv()
            c["ax"] = go(z, rx, A, side)
            c["bm0"] = go(z, rx, B, up)
            c["bp0"] = go(z, rx, B, down)
            c["am0"] = go(z, rx, A, up)
            c["ap0"] = go(z, rx, A, down)
            c["bx0"] = go(z, rx, B, side)

        def g2():
            c["bm0"].wait_recv()
            c["bm1"] = go(zm, rx, BL, up)
            c["bx1"] = go(zm, rx, B, side)
            c["bp0"].wait_recv()
            c["bp1"] = go(zp, rx, BR, down)
            c["bx2"] = go(zp, rx, B, side)
            c["ax"].wait_recv()
            c["am1"] = go(z, 1 - rx, A, up)
            c["ap1"] = go(z, 1 - rx, A, down)
            c["am0"].wait_recv()
            c["am2"] = go(zm, rx, A, up)

        def g3():
            c["bm1"].wait_recv()
            c["bx3"] = go(z2, rx, BL, side)
            c["bp1"].wait_recv()
            c["bx4"] = go(z2, rx, BR, side)
            c["ap1"].wait_recv()
            c["ap2"] = go(zp, 1 - rx, A, down)

        def g4():
            for name in ("ap0", "am1", "am2", "ap2", "bx0", "bx1", "bx2", "bx3", "bx4"):
                c[name].wait_recv()

        return shift, g1, g2, g3, g4

    fa, fb, fs1, fs2, fs3, fs4 = scatter(fv, ra_f, rbx_f, rbz_f, total)
    ba, bb, bs1, bs2, bs3, bs4 = scatter(sv, ra_b, rbx_b, rbz_b, total)
    f_shift, fg1, fg2, fg3, fg4 = gather(of, stage_f, after, held_f)
    b_shift, bg1, bg2, bg3, bg4 = gather(ob, stage_b, before, held_b)

    l_fin.wait()
    scales(fv)

    def normed_front(n):
        cols = tile(n)
        y = dot(fv[:, cols], had[...])
        column = signs(cols) * gain[pl.ds(front, 1), cols] * UNIT
        s = rows_scale[...]
        fv[:, cols] = (y * column * jnp.concatenate([s, s], axis=1)).astype(BF16)
    loop(D // TILE, normed_front)
    l_wk.wait()
    l_wv.wait()
    q_step = project(fv, front)
    l_wq.wait()
    loop(2, q_step)

    def attend(h):
        cols = tile(h, HD)
        for lo in (0, 256):
            rows = pl.ds(lo, 256)
            probs = probabilities(qv[rows, cols], lo, 256).astype(BF16)
            ctx[rows, cols] = dot(probs, kvv[pl.ds(0, lo + 256), pl.ds(HD, HD)]).astype(BF16)
    loop(HEADS, attend)
    l_wo.wait()

    def project_out(n):
        cols = tile(n)
        fv[:, cols] = dot(ctx[...], wov[front, :, cols]).astype(BF16)
    loop(CA // TILE, project_out)
    pl.semaphore_wait(barrier, 5)
    fa()
    loop(CB // TILE, lambda n: project_out(n + CA // TILE))
    fb()

    l_sav.wait()
    scales(sv)

    def normed_back(n):
        cols = tile(n)
        s = rows_scale[...]
        sv[:, cols] = (
            sv[:, cols].astype(F32) * gain[pl.ds(back, 1), cols] * jnp.concatenate([s, s], axis=1)
        ).astype(BF16)
    loop(D // TILE, normed_back)
    q_step = project(sv, back)
    loop(2, q_step)
    fs1()
    l_gin.wait()

    def unrotated(n):
        cols = tile(n)
        gv[:, cols] = (dot(gv[:, cols], had[...]) * (signs(cols) * UNIT)).astype(BF16)
    loop(D // TILE, unrotated)

    def pull_out(n):
        rows = tile(n)
        dctx[:, rows] = dot_nt(gv[...], wov[back, rows, :]).astype(BF16)
    loop(2, pull_out)
    dkv[...] = jnp.zeros_like(dkv)

    def attend_back(h):
        cols = tile(h, HD)
        for lo in (0, 256):
            rows, n = pl.ds(lo, 256), pl.ds(0, lo + 256)
            q, d = qv[rows, cols], dctx[rows, cols]
            probs = probabilities(q, lo, 256)
            dkv[n, pl.ds(HD, HD)] += dot_tn(probs.astype(BF16), d)
            dp = dot_nt(d, kvv[n, pl.ds(HD, HD)])
            ds = probs * (dp - jnp.sum(probs * dp, axis=-1, keepdims=True)) * SM
            ds = ds.astype(BF16)
            dq[rows, cols] = dot(ds, kvv[n, pl.ds(0, HD)]).astype(BF16)
            dkv[n, pl.ds(0, HD)] += dot_tn(ds, q)
    loop(HEADS, attend_back)
    dkvb[...] = dkv[...].astype(BF16)
    fs2()

    def pull_in(n):
        cols = tile(n)
        sv[:, cols] = (dot_nt(dq[...], wqv[back, cols, :]) + dot_nt(dkvb[...], wkv[back, cols, :])).astype(BF16)
    loop(CA // TILE, pull_in)
    ba()
    loop(CB // TILE, lambda n: pull_in(n + CA // TILE))
    bb()

    fs3()
    bs1()
    fs4()
    l_fr.wait()
    turn(total, fr, stage_f)
    f_shift()
    bs2()
    fg1()
    bs3()
    fg2()
    bs4()
    l_sr.wait()
    l_gr.wait()

    def norm_back(i):
        rows = tile(i, 16)
        v = sr[rows, :].astype(F32)
        s = lax.rsqrt(jnp.sum(v * v, axis=-1, keepdims=True) * (1.0 / D) + EPS)
        g = total[rows, :] * gain[pl.ds(back, 1), :]
        inner = jnp.sum(v * g, axis=-1, keepdims=True)
        total[rows, :] = s * g - v * (s * s * s * inner * (1.0 / D))
    loop(BLOCK // 16, norm_back)
    turn(total, gr, stage_b)
    b_shift()
    fg3()
    bg1()
    fg4()
    bg2()
    bg3()
    bg4()
    for copy in started:
        copy.wait_send()


def local(forward_input, saved_input, gradient_input, roster, sign_bits, gain, w_query, w_key, w_value, w_out):
    vm = lambda shape, kind=BF16: pltpu.VMEM(shape, kind)
    anywhere = pl.BlockSpec(memory_space=pl.ANY)
    inside = pl.BlockSpec(memory_space=pltpu.VMEM)
    sums = [vm((7, BLOCK, CA)), vm((4, BLOCK, CB)), vm((6, BLOCK, HALF))]
    out = jax.ShapeDtypeStruct((ROWS, D), BF16)
    arrived, returned = pl.pallas_call(
        kernel,
        out_shape=(out, out),
        in_specs=[pl.BlockSpec(memory_space=pltpu.SMEM), inside, inside] + [anywhere] * 7,
        out_specs=(anywhere, anywhere),
        scratch_shapes=[
            vm((ROWS, D)), vm((ROWS, D)), vm((ROWS, D)),
            vm((2, D, HEADS * HD)), vm((2, D, 2 * HD)), vm((2, HEADS * HD, D)),
            vm((BLOCK, D)), vm((BLOCK, D)), vm((BLOCK, D)),
            vm((2 * HB, 2 * HB)), vm((ROWS, 128), F32),
            vm((ROWS, HEADS * HD)), vm((ROWS, 2 * HD)), vm((ROWS, HEADS * HD)), vm((ROWS, HEADS * HD)),
            vm((ROWS, HEADS * HD)), vm((ROWS, 2 * HD), F32), vm((ROWS, 2 * HD)),
            *sums, *sums, vm((BLOCK, D), F32), vm((BLOCK, D)), vm((BLOCK, D)),
            pltpu.SemaphoreType.DMA((10,)), pltpu.SemaphoreType.DMA((68,)), pltpu.SemaphoreType.DMA((68,)),
        ],
        compiler_params=pltpu.CompilerParams(
            collective_id=0, has_side_effects=True, vmem_limit_bytes=60 * 2**20
        ),
        cost_estimate=pl.CostEstimate(flops=16 * 10**9, bytes_accessed=45 * 10**6, transcendentals=2 * 10**6),
        name="relay_slot",
    )(
        roster[0], sign_bits[None], gain[0], forward_input[0], saved_input[0], gradient_input[0],
        w_query[0], w_key[0], w_value[0], w_out[0],
    )
    return (arrived[None], returned[None])


def solution(mesh):
    placed = (
        P("pipe", None, None),
        P("pipe", None, None),
        P("pipe", None, None),
        P("pipe", None),
        P(),
        P("pipe", None, None),
        P("pipe", None, None, "tensor"),
        P("pipe", None, None, "tensor"),
        P("pipe", None, None, "tensor"),
        P("pipe", None, "tensor", None),
    )
    return jax.shard_map(
        local,
        mesh=mesh,
        in_specs=placed,
        out_specs=(P("pipe", None, None), P("pipe", None, None)),
        check_vma=False,
    )
```

time: 638 us -> 158 us (0.25); the launches traced: 628 us -> 158 us
  waiting for transfers between devices: 404 us -> 0 us
  Pallas kernels: 0 us -> 151 us
  matrix products: 116 us -> 0 us
  other arithmetic: 41.7 us -> 0 us
  local copies, waits for them, and re-layouts: 45.1 us -> 6.87 us
  between operations: 18.7 us -> 0.65 us
    psum x1 -> x0, waiting for transfers between devices: 317 us -> none  [local(): lax.psum(partial_out.astype(jnp.bfloat16), 'tensor').astype(jnp.float32)]
    pallas_call x0 -> x1, Pallas kernels: none -> 151 us  [local(): pl.pallas_call(kernel, out_shape=(out, out), in_specs=[pl.BlockSpec(memor...]
    dot_general x17 -> x0, matrix products: 116 us -> none  [the longest x2 23 us: rotate(): jnp.einsum('rbk,kj->rbj', blocks, hadamard(HB), precision=lax.Precision.H...]
    ppermute x2 -> x0, waiting for transfers between devices: 86.2 us -> none  [shifted(): return lax.ppermute(value, axis, pairs)]
    reshape x2 -> x0, local copies, waits for them, and re-layouts: 17.9 us -> none  [unrotate(): return (turned / math.sqrt(HB)).reshape(count, -1) * signs]
    unnamed x3 -> x0, other arithmetic: 13.6 us -> none
    convert_element_type x2 -> x0, local copies, waits for them, and re-layouts: 12.6 us -> none  [the longest x1 6.32 us: local(): sent_activation = rotate(inputs + mixed, signs).astype(jnp.bfloat16)]
    div x5 -> x0, other arithmetic: 12.5 us -> none  [the longest x2 12.5 us: unrotate(): return (turned / math.sqrt(HB)).reshape(count, -1) * signs]
  transfers between devices with their start and end apart: 3 -> 0, of which waited for: 3 -> 0; matrix products, arithmetic and copies ran while one was open for 5% -> 0% of each run, Pallas kernels for 0% -> 0%
where the time goes in v1:
time: 158 us
  Pallas kernels  151 us (96%)
  local copies, waits for them, and re-layouts  6.87 us (4%)
    pallas_call x1, Pallas kernels, local(): pl.pallas_call(kernel, out_shape=(out, out), in_specs=[pl.BlockSpec(memor...  151 us
    unnamed x4, local copies, waits for them, and re-layouts  6.87 us

profile of v1, /device:TPU:1, one launch (start us, length us, event | category | flops | bytes accessed | tf_op | source)
XLA Modules:
  0.0 158.1 jit_solution(3559948505729334466)
XLA Ops:
  0.6 150.5 %relay_slot.1 = (bf16[512,4096]{1,0:T(8,128)(2,1)}, bf16[512,4096]{1,0:T(8,128)(2,1)}) custom-call(s32[2]{0:T(128)} %bitcast.23, s32[1,4096]{1,0:T(1,128)} %bitcast.22, f32[2,4096]{1,0:T(2,128)} %bitcast.21, bf16[512,4096]{1,0:T(8,128)(2,1)} %bitcast.16, bf16[512,4096]{1,0:T(8,128)(2,1)} %bitcast.17, bf16[512,4096]{1,0:T(8,128)(2,1)} %bitcast.18, ...), custom_call_target="tpu_custom_call" | custom-call | flops 16000000000 | bytes 45000000 | tf_op jit(solution)/shard_map/relay_slot/pallas_call | solution.py:407
  151.2 0.0 copy-start
  151.2 4.8 %copy.14 = bf16[1,512,4096]{2,1,0:T(8,128)(2,1)} copy(bf16[1,512,4096]{2,1,0:T(8,128)(2,1)} %bitcast.13) | data formatting | bytes 8388608
  156.0 0.0 copy-done
  156.0 2.0 %copy.15 = bf16[1,512,4096]{2,1,0:T(8,128)(2,1)} copy(bf16[1,512,4096]{2,1,0:T(8,128)(2,1)S(1)} %bitcast.12) | data formatting | bytes 8388608
Async XLA Ops:
  151.2 4.9 %copy-start = (bf16[512,4096]{1,0:T(8,128)(2,1)S(1)}, bf16[512,4096]{1,0:T(8,128)(2,1)}, u32[]{:S(2)}) copy-start(bf16[512,4096]{1,0:T(8,128)(2,1)} %get-tuple-element.5) | copy-start | bytes 12582916

commit v2 on v1

--- a/solution.py
+++ b/solution.py
@@ -46,8 +46,8 @@
     return pl.ds(pl.multiple_of(c * width, width), width)
 
 
-def loop(count, body):
-    lax.fori_loop(0, count, lambda i, _: (body(i), 0)[1], 0)
+def loop(count, body, unroll=1, start=0):
+    lax.fori_loop(start, start + count, lambda i, _: (body(i), 0)[1], 0, unroll=unroll)
 
 
 def hadamard_pair():
@@ -88,13 +88,15 @@
 
     mine = block(t)
     loads = [
-        (fin, fv), (wk, wkv.at[:, :, pl.ds(0, HD)]), (wv, wkv.at[:, :, pl.ds(HD, HD)]), (wq, wqv), (wo, wov),
+        (wk, wkv.at[:, :, pl.ds(0, HD)]), (wv, wkv.at[:, :, pl.ds(HD, HD)]), (wq, wqv), (wo, wov),
         (sav, sv), (gin, gv), (fin.at[mine], fr), (sav.at[mine], sr), (gin.at[mine], gr),
     ]
+    quarters = [pl.ds(i * 128, 128) for i in range(4)]
+    loads += [(fin.at[rows], fv.at[rows]) for rows in quarters]
     loads = [pltpu.make_async_copy(a, b, load.at[i]) for i, (a, b) in enumerate(loads)]
-    for one in loads:
+    l_wk, l_wv, l_wq, l_wo, l_sav, l_gin, l_fr, l_sr, l_gr, *l_fin = loads
+    for one in (*l_fin, l_wk, l_wv, l_wq):
         one.start()
-    l_fin, l_wk, l_wv, l_wq, l_wo, l_sav, l_gin, l_fr, l_sr, l_gr = loads
 
     barrier = pltpu.get_barrier_semaphore()
     for other in (up, down, side, after, before):
@@ -119,29 +121,26 @@
         started.append(copy)
         return copy
 
-    def scales(ref):
-        def body(i):
-            rows = tile(i, 32)
-            v = ref[rows, :].astype(F32)
-            s = lax.rsqrt(jnp.sum(v * v, axis=-1, keepdims=True) * (1.0 / D) + EPS)
-            rows_scale[rows, :] = jnp.broadcast_to(s, (32, 128))
-        loop(ROWS // 32, body)
+    def scales(factor):
+        total_square = jnp.sum(rows_scale[...], axis=-1, keepdims=True)
+        rows_scale[...] = jnp.broadcast_to(lax.rsqrt(total_square * (factor / D) + EPS), (ROWS, 128))
 
     def project(ref, which):
-        kvv[...] = dot(ref[...], wkv[which]).astype(BF16)
-        def body(n):
-            cols = tile(n)
-            qv[:, cols] = dot(ref[...], wqv[which, :, cols]).astype(BF16)
-        return body
-
-    def probabilities(q, lo, size):
+        s = rows_scale[...]
+        s2 = jnp.concatenate([s, s], axis=1)
+        kvv[...] = (dot(ref[...], wkv[which]) * s2).astype(BF16)
+        for n in range(2):
+            cols = pl.ds(n * TILE, TILE)
+            qv[:, cols] = (dot(ref[...], wqv[which, :, cols]) * (s2 * SM)).astype(BF16)
+
+    def weights(q, lo, size):
         n = lo + size
-        s = dot_nt(q, kvv[pl.ds(0, n), pl.ds(0, HD)]) * SM
+        s = dot_nt(q, kvv[pl.ds(0, n), pl.ds(0, HD)])
         row = lax.broadcasted_iota(jnp.int32, (size, n), 0) + lo
         col = lax.broadcasted_iota(jnp.int32, (size, n), 1)
         s = jnp.where(row >= col, s, -1e30)
         e = jnp.exp(s - jnp.max(s, axis=-1, keepdims=True))
-        return e / jnp.sum(e, axis=-1, keepdims=True)
+        return e, 1.0 / jnp.sum(e, axis=-1, keepdims=True)
 
     def add(ref, base, cols, *terms):
         def body(i):
@@ -172,6 +171,8 @@
             c["p0"].wait_recv()
             add(part, 2 * zm + 1, A, ra.at[1])
             c["p2"] = push(part.at[block(2 * zm + 1), A], ra.at[5], down)
+
+        def s1x():
             c["x", 2].wait_recv()
             add(part, 2 * z2 + x, B, rbx.at[2])
             c["bm0"] = push(part.at[block(2 * z2 + x), BL], rbz.at[0], up)
@@ -181,12 +182,14 @@
             c["x", 1].wait_recv()
             add(part, 2 * zp + x, B, rbx.at[1])
             c["bm1"] = push(part.at[block(2 * zp + x), BR], rbz.at[2], up)
+            c["bm0"].wait_recv()
+            add(part, 2 * zp + x, BL, rbz.at[0])
+            c["bm2"] = push(part.at[block(2 * zp + x), BL], rbz.at[4], up)
+
+        def s2x():
             c["x", 3].wait_recv()
             add(part, 2 * zm + x, B, rbx.at[3])
             c["bp1"] = push(part.at[block(2 * zm + x), BL], rbz.at[3], down)
-            c["bm0"].wait_recv()
-            add(part, 2 * zp + x, BL, rbz.at[0])
-            c["bm2"] = push(part.at[block(2 * zp + x), BL], rbz.at[4], up)
             c["bp0"].wait_recv()
             add(part, 2 * zm + x, BR, rbz.at[1])
             c["bp2"] = push(part.at[block(2 * zm + x), BR], rbz.at[5], down)
@@ -216,7 +219,7 @@
                 )
             loop(BLOCK // 16, body)
 
-        return first_a, first_b, s1, s2, s3, s4
+        return first_a, first_b, s1, s1x, s2, s2x, s3, s4
 
     def turn(whole, held, stage):
         def body(n):
@@ -226,7 +229,7 @@
             lo = (v - hi.astype(F32)).astype(BF16)
             y = dot(hi, had[...]) + dot(lo, had[...])
             stage[:, cols] = (held[:, cols].astype(F32) + y * UNIT).astype(BF16)
-        loop(D // TILE, body)
+        loop(D // TILE, body, 4)
 
     def gather(out, stage, device, r):
         c = {}
@@ -275,105 +278,115 @@
 
         return shift, g1, g2, g3, g4
 
-    fa, fb, fs1, fs2, fs3, fs4 = scatter(fv, ra_f, rbx_f, rbz_f, total)
-    ba, bb, bs1, bs2, bs3, bs4 = scatter(sv, ra_b, rbx_b, rbz_b, total)
+    fa, fb, fs1, fs1x, fs2, fs2x, fs3, fs4 = scatter(fv, ra_f, rbx_f, rbz_f, total)
+    ba, bb, bs1, bs1x, bs2, bs2x, bs3, bs4 = scatter(sv, ra_b, rbx_b, rbz_b, total)
     f_shift, fg1, fg2, fg3, fg4 = gather(of, stage_f, after, held_f)
     b_shift, bg1, bg2, bg3, bg4 = gather(ob, stage_b, before, held_b)
 
-    l_fin.wait()
-    scales(fv)
-
-    def normed_front(n):
+    rows_scale[...] = jnp.zeros_like(rows_scale)
+    for one in l_fin:
+        one.wait()
+    l_wo.start()
+
+    def weighted_front(n):
         cols = tile(n)
         y = dot(fv[:, cols], had[...])
-        column = signs(cols) * gain[pl.ds(front, 1), cols] * UNIT
-        s = rows_scale[...]
-        fv[:, cols] = (y * column * jnp.concatenate([s, s], axis=1)).astype(BF16)
-    loop(D // TILE, normed_front)
+        fv[:, cols] = (y * (signs(cols) * gain[pl.ds(front, 1), cols] * UNIT)).astype(BF16)
+        y = y * y
+        rows_scale[...] += y[:, :128] + y[:, 128:]
+    loop(D // TILE, weighted_front, 4)
+    scales(1.0 / HB)
     l_wk.wait()
     l_wv.wait()
-    q_step = project(fv, front)
     l_wq.wait()
-    loop(2, q_step)
-
-    def attend(h):
-        cols = tile(h, HD)
+    for one in (l_sav, l_gin, l_fr, l_sr, l_gr):
+        one.start()
+    project(fv, front)
+
+    for h in range(HEADS):
+        cols = pl.ds(h * HD, HD)
         for lo in (0, 256):
             rows = pl.ds(lo, 256)
-            probs = probabilities(qv[rows, cols], lo, 256).astype(BF16)
-            ctx[rows, cols] = dot(probs, kvv[pl.ds(0, lo + 256), pl.ds(HD, HD)]).astype(BF16)
-    loop(HEADS, attend)
+            e, r = weights(qv[rows, cols], lo, 256)
+            ctx[rows, cols] = (dot(e.astype(BF16), kvv[pl.ds(0, lo + 256), pl.ds(HD, HD)]) * r).astype(BF16)
     l_wo.wait()
 
     def project_out(n):
         cols = tile(n)
         fv[:, cols] = dot(ctx[...], wov[front, :, cols]).astype(BF16)
-    loop(CA // TILE, project_out)
+    loop(CA // TILE, project_out, 3)
     pl.semaphore_wait(barrier, 5)
     fa()
-    loop(CB // TILE, lambda n: project_out(n + CA // TILE))
+    loop(CB // TILE, project_out, 7, CA // TILE)
     fb()
 
+    rows_scale[...] = jnp.zeros_like(rows_scale)
     l_sav.wait()
-    scales(sv)
-
-    def normed_back(n):
+
+    def weighted_back(n):
         cols = tile(n)
-        s = rows_scale[...]
-        sv[:, cols] = (
-            sv[:, cols].astype(F32) * gain[pl.ds(back, 1), cols] * jnp.concatenate([s, s], axis=1)
-        ).astype(BF16)
-    loop(D // TILE, normed_back)
-    q_step = project(sv, back)
-    loop(2, q_step)
+        v = sv[:, cols].astype(F32)
+        sv[:, cols] = (v * gain[pl.ds(back, 1), cols]).astype(BF16)
+        v = v * v
+        rows_scale[...] += v[:, :128] + v[:, 128:]
+    loop(D // TILE, weighted_back, 4)
+    scales(1.0)
+    project(sv, back)
     fs1()
+    fs1x()
     l_gin.wait()
 
     def unrotated(n):
         cols = tile(n)
         gv[:, cols] = (dot(gv[:, cols], had[...]) * (signs(cols) * UNIT)).astype(BF16)
-    loop(D // TILE, unrotated)
-
-    def pull_out(n):
-        rows = tile(n)
+    loop(D // TILE, unrotated, 4)
+
+    for n in range(2):
+        rows = pl.ds(n * TILE, TILE)
         dctx[:, rows] = dot_nt(gv[...], wov[back, rows, :]).astype(BF16)
-    loop(2, pull_out)
+    fs2()
     dkv[...] = jnp.zeros_like(dkv)
 
     def attend_back(h):
-        cols = tile(h, HD)
+        cols = pl.ds(h * HD, HD)
         for lo in (0, 256):
             rows, n = pl.ds(lo, 256), pl.ds(0, lo + 256)
             q, d = qv[rows, cols], dctx[rows, cols]
-            probs = probabilities(q, lo, 256)
-            dkv[n, pl.ds(HD, HD)] += dot_tn(probs.astype(BF16), d)
+            e, r = weights(q, lo, 256)
+            probs = e * r
+            dkv[pl.ds(HD, HD), n] += dot_tn(d, probs.astype(BF16))
             dp = dot_nt(d, kvv[n, pl.ds(HD, HD)])
-            ds = probs * (dp - jnp.sum(probs * dp, axis=-1, keepdims=True)) * SM
-            ds = ds.astype(BF16)
-            dq[rows, cols] = dot(ds, kvv[n, pl.ds(0, HD)]).astype(BF16)
-            dkv[n, pl.ds(0, HD)] += dot_tn(ds, q)
-    loop(HEADS, attend_back)
+            ds = (probs * (dp - jnp.sum(probs * dp, axis=-1, keepdims=True))).astype(BF16)
+            dq[rows, cols] = (dot(ds, kvv[n, pl.ds(0, HD)]) * SM).astype(BF16)
+            dkv[pl.ds(0, HD), n] += dot_tn(q, ds)
+    attend_back(0)
+    attend_back(1)
+    fs2x()
+    attend_back(2)
+    attend_back(3)
     dkvb[...] = dkv[...].astype(BF16)
-    fs2()
+    fs3()
 
     def pull_in(n):
         cols = tile(n)
-        sv[:, cols] = (dot_nt(dq[...], wqv[back, cols, :]) + dot_nt(dkvb[...], wkv[back, cols, :])).astype(BF16)
-    loop(CA // TILE, pull_in)
+        sv[:, cols] = (dot_nt(dq[...], wqv[back, cols, :]) + dot_nt(dkvb[...].T, wkv[back, cols, :])).astype(BF16)
+    loop(CA // TILE, pull_in, 3)
     ba()
-    loop(CB // TILE, lambda n: pull_in(n + CA // TILE))
+    loop(CB // TILE, pull_in, 7, CA // TILE)
     bb()
 
-    fs3()
-    bs1()
     fs4()
     l_fr.wait()
     turn(total, fr, stage_f)
     f_shift()
+    bs1()
+    bs1x()
     bs2()
     fg1()
+    bs2x()
+    fg2()
     bs3()
-    fg2()
+    fg3()
     bs4()
     l_sr.wait()
     l_gr.wait()
@@ -388,7 +401,6 @@
     loop(BLOCK // 16, norm_back)
     turn(total, gr, stage_b)
     b_shift()
-    fg3()
     bg1()
     fg4()
     bg2()
@@ -415,9 +427,9 @@
             vm((BLOCK, D)), vm((BLOCK, D)), vm((BLOCK, D)),
             vm((2 * HB, 2 * HB)), vm((ROWS, 128), F32),
             vm((ROWS, HEADS * HD)), vm((ROWS, 2 * HD)), vm((ROWS, HEADS * HD)), vm((ROWS, HEADS * HD)),
-            vm((ROWS, HEADS * HD)), vm((ROWS, 2 * HD), F32), vm((ROWS, 2 * HD)),
+            vm((ROWS, HEADS * HD)), vm((2 * HD, ROWS), F32), vm((2 * HD, ROWS)),
             *sums, *sums, vm((BLOCK, D), F32), vm((BLOCK, D)), vm((BLOCK, D)),
-            pltpu.SemaphoreType.DMA((10,)), pltpu.SemaphoreType.DMA((68,)), pltpu.SemaphoreType.DMA((68,)),
+            pltpu.SemaphoreType.DMA((13,)), pltpu.SemaphoreType.DMA((68,)), pltpu.SemaphoreType.DMA((68,)),
         ],
         compiler_params=pltpu.CompilerParams(
             collective_id=0, has_side_effects=True, vmem_limit_bytes=60 * 2**20

time: 158 us -> 147 us (0.930)
  Pallas kernels: 151 us -> 139 us
    pallas_call x1, Pallas kernels: 151 us -> 139 us  [local(): pl.pallas_call(kernel, out_shape=(out, out), in_specs=[pl.BlockSpec(memor...]
where the time goes in v2:
time: 147 us
  Pallas kernels  139 us (95%)
  local copies, waits for them, and re-layouts  6.87 us (5%)
    pallas_call x1, Pallas kernels, local(): pl.pallas_call(kernel, out_shape=(out, out), in_specs=[pl.BlockSpec(memor...  139 us
    unnamed x4, local copies, waits for them, and re-layouts  6.87 us

profile of v2, /device:TPU:1, one launch (start us, length us, event | category | flops | bytes accessed | tf_op | source)
XLA Modules:
  0.0 146.8 jit_solution(2715476546390077117)
XLA Ops:
  0.6 139.3 %relay_slot.1 = (bf16[512,4096]{1,0:T(8,128)(2,1)}, bf16[512,4096]{1,0:T(8,128)(2,1)}) custom-call(s32[2]{0:T(128)} %bitcast.23, s32[1,4096]{1,0:T(1,128)} %bitcast.22, f32[2,4096]{1,0:T(2,128)} %bitcast.21, bf16[512,4096]{1,0:T(8,128)(2,1)} %bitcast.16, bf16[512,4096]{1,0:T(8,128)(2,1)} %bitcast.17, bf16[512,4096]{1,0:T(8,128)(2,1)} %bitcast.18, ...), custom_call_target="tpu_custom_call" | custom-call | flops 16000000000 | bytes 45000000 | tf_op jit(solution)/shard_map/relay_slot/pallas_call | solution.py:419
  140.0 0.0 copy-start
  140.0 4.8 %copy.14 = bf16[1,512,4096]{2,1,0:T(8,128)(2,1)} copy(bf16[1,512,4096]{2,1,0:T(8,128)(2,1)} %bitcast.13) | data formatting | bytes 8388608
  144.8 0.0 copy-done
  144.8 2.0 %copy.15 = bf16[1,512,4096]{2,1,0:T(8,128)(2,1)} copy(bf16[1,512,4096]{2,1,0:T(8,128)(2,1)S(1)} %bitcast.12) | data formatting | bytes 8388608
Async XLA Ops:
  140.0 4.9 %copy-start = (bf16[512,4096]{1,0:T(8,128)(2,1)S(1)}, bf16[512,4096]{1,0:T(8,128)(2,1)}, u32[]{:S(2)}) copy-start(bf16[512,4096]{1,0:T(8,128)(2,1)} %get-tuple-element.5) | copy-start | bytes 12582916

commit v3 on v2

--- a/solution.py
+++ b/solution.py
@@ -286,7 +286,6 @@
     rows_scale[...] = jnp.zeros_like(rows_scale)
     for one in l_fin:
         one.wait()
-    l_wo.start()
 
     def weighted_front(n):
         cols = tile(n)
@@ -295,13 +294,14 @@
         y = y * y
         rows_scale[...] += y[:, :128] + y[:, 128:]
     loop(D // TILE, weighted_front, 4)
+    l_wo.start()
     scales(1.0 / HB)
     l_wk.wait()
     l_wv.wait()
     l_wq.wait()
+    project(fv, front)
     for one in (l_sav, l_gin, l_fr, l_sr, l_gr):
         one.start()
-    project(fv, front)
 
     for h in range(HEADS):
         cols = pl.ds(h * HD, HD)
@@ -322,6 +322,7 @@
 
     rows_scale[...] = jnp.zeros_like(rows_scale)
     l_sav.wait()
+    l_gin.wait()
 
     def weighted_back(n):
         cols = tile(n)
@@ -329,18 +330,12 @@
         sv[:, cols] = (v * gain[pl.ds(back, 1), cols]).astype(BF16)
         v = v * v
         rows_scale[...] += v[:, :128] + v[:, 128:]
+        gv[:, cols] = (dot(gv[:, cols], had[...]) * (signs(cols) * UNIT)).astype(BF16)
     loop(D // TILE, weighted_back, 4)
     scales(1.0)
     project(sv, back)
     fs1()
     fs1x()
-    l_gin.wait()
-
-    def unrotated(n):
-        cols = tile(n)
-        gv[:, cols] = (dot(gv[:, cols], had[...]) * (signs(cols) * UNIT)).astype(BF16)
-    loop(D // TILE, unrotated, 4)
-
     for n in range(2):
         rows = pl.ds(n * TILE, TILE)
         dctx[:, rows] = dot_nt(gv[...], wov[back, rows, :]).astype(BF16)
@@ -382,11 +377,9 @@
     bs1()
     bs1x()
     bs2()
+    bs2x()
+    bs3()
     fg1()
-    bs2x()
-    fg2()
-    bs3()
-    fg3()
     bs4()
     l_sr.wait()
     l_gr.wait()
@@ -401,6 +394,8 @@
     loop(BLOCK // 16, norm_back)
     turn(total, gr, stage_b)
     b_shift()
+    fg2()
+    fg3()
     bg1()
     fg4()
     bg2()
@@ -415,12 +410,12 @@
     anywhere = pl.BlockSpec(memory_space=pl.ANY)
     inside = pl.BlockSpec(memory_space=pltpu.VMEM)
     sums = [vm((7, BLOCK, CA)), vm((4, BLOCK, CB)), vm((6, BLOCK, HALF))]
-    out = jax.ShapeDtypeStruct((ROWS, D), BF16)
+    out = pltpu.VMEM((ROWS, D), BF16)
     arrived, returned = pl.pallas_call(
         kernel,
         out_shape=(out, out),
         in_specs=[pl.BlockSpec(memory_space=pltpu.SMEM), inside, inside] + [anywhere] * 7,
-        out_specs=(anywhere, anywhere),
+        out_specs=(inside, inside),
         scratch_shapes=[
             vm((ROWS, D)), vm((ROWS, D)), vm((ROWS, D)),
             vm((2, D, HEADS * HD)), vm((2, D, 2 * HD)), vm((2, HEADS * HD, D)),
@@ -432,7 +427,7 @@
             pltpu.SemaphoreType.DMA((13,)), pltpu.SemaphoreType.DMA((68,)), pltpu.SemaphoreType.DMA((68,)),
         ],
         compiler_params=pltpu.CompilerParams(
-            collective_id=0, has_side_effects=True, vmem_limit_bytes=60 * 2**20
+            collective_id=0, has_side_effects=True, vmem_limit_bytes=51 * 2**20
         ),
         cost_estimate=pl.CostEstimate(flops=16 * 10**9, bytes_accessed=45 * 10**6, transcendentals=2 * 10**6),
         name="relay_slot",

time: 147 us -> 140 us (0.952)
  Pallas kernels: 139 us -> 135 us
  local copies, waits for them, and re-layouts: 6.87 us -> 4.03 us
    pallas_call x1, Pallas kernels: 139 us -> 135 us  [local(): pl.pallas_call(kernel, out_shape=(out, out), in_specs=[pl.BlockSpec(memor...]
    unnamed x4 -> x2, local copies, waits for them, and re-layouts: 6.87 us -> 4.03 us
where the time goes in v3:
time: 140 us; the launch traced here: 139 us
  Pallas kernels  135 us (96%)
  local copies, waits for them, and re-layouts  4.03 us (3%)
    pallas_call x1, Pallas kernels, local(): pl.pallas_call(kernel, out_shape=(out, out), in_specs=[pl.BlockSpec(memor...  135 us
    unnamed x2, local copies, waits for them, and re-layouts  4.03 us

profile of v3, /device:TPU:1, one launch (start us, length us, event | category | flops | bytes accessed | tf_op | source)
XLA Modules:
  0.0 139.4 jit_solution(11767796670095058668)
XLA Ops:
  0.6 134.8 %relay_slot.1 = (bf16[512,4096]{1,0:T(8,128)(2,1)S(1)}, bf16[512,4096]{1,0:T(8,128)(2,1)S(1)}) custom-call(s32[2]{0:T(128)} %bitcast.23, s32[1,4096]{1,0:T(1,128)} %bitcast.22, f32[2,4096]{1,0:T(2,128)} %bitcast.21, bf16[512,4096]{1,0:T(8,128)(2,1)} %bitcast.16, bf16[512,4096]{1,0:T(8,128)(2,1)} %bitcast.17, bf16[512,4096]{1,0:T(8,128)(2,1)} %bitcast.18, ...), custom_call_target="tpu_custom_call" | custom-call | flops 16000000000 | bytes 45000000 | tf_op jit(solution)/shard_map/relay_slot/pallas_call | solution.py:414
  135.4 2.0 %copy.14 = bf16[1,512,4096]{2,1,0:T(8,128)(2,1)} copy(bf16[1,512,4096]{2,1,0:T(8,128)(2,1)S(1)} %bitcast.13) | data formatting | bytes 8388608
  137.4 2.0 %copy.15 = bf16[1,512,4096]{2,1,0:T(8,128)(2,1)} copy(bf16[1,512,4096]{2,1,0:T(8,128)(2,1)S(1)} %bitcast.12) | data formatting | bytes 8388608

commit v4 on v3

--- a/solution.py
+++ b/solution.py
@@ -182,14 +182,16 @@
             c["x", 1].wait_recv()
             add(part, 2 * zp + x, B, rbx.at[1])
             c["bm1"] = push(part.at[block(2 * zp + x), BR], rbz.at[2], up)
-            c["bm0"].wait_recv()
-            add(part, 2 * zp + x, BL, rbz.at[0])
-            c["bm2"] = push(part.at[block(2 * zp + x), BL], rbz.at[4], up)
 
         def s2x():
             c["x", 3].wait_recv()
             add(part, 2 * zm + x, B, rbx.at[3])
             c["bp1"] = push(part.at[block(2 * zm + x), BL], rbz.at[3], down)
+
+        def s2z():
+            c["bm0"].wait_recv()
+            add(part, 2 * zp + x, BL, rbz.at[0])
+            c["bm2"] = push(part.at[block(2 * zp + x), BL], rbz.at[4], up)
             c["bp0"].wait_recv()
             add(part, 2 * zm + x, BR, rbz.at[1])
             c["bp2"] = push(part.at[block(2 * zm + x), BR], rbz.at[5], down)
@@ -219,7 +221,7 @@
                 )
             loop(BLOCK // 16, body)
 
-        return first_a, first_b, s1, s1x, s2, s2x, s3, s4
+        return first_a, first_b, s1, s1x, s2, s2x, s2z, s3, s4
 
     def turn(whole, held, stage):
         def body(n):
@@ -278,8 +280,8 @@
 
         return shift, g1, g2, g3, g4
 
-    fa, fb, fs1, fs1x, fs2, fs2x, fs3, fs4 = scatter(fv, ra_f, rbx_f, rbz_f, total)
-    ba, bb, bs1, bs1x, bs2, bs2x, bs3, bs4 = scatter(sv, ra_b, rbx_b, rbz_b, total)
+    fa, fb, fs1, fs1x, fs2, fs2x, fs2z, fs3, fs4 = scatter(fv, ra_f, rbx_f, rbz_f, total)
+    ba, bb, bs1, bs1x, bs2, bs2x, bs2z, bs3, bs4 = scatter(sv, ra_b, rbx_b, rbz_b, total)
     f_shift, fg1, fg2, fg3, fg4 = gather(of, stage_f, after, held_f)
     b_shift, bg1, bg2, bg3, bg4 = gather(ob, stage_b, before, held_b)
 
@@ -333,9 +335,9 @@
         gv[:, cols] = (dot(gv[:, cols], had[...]) * (signs(cols) * UNIT)).astype(BF16)
     loop(D // TILE, weighted_back, 4)
     scales(1.0)
-    project(sv, back)
     fs1()
     fs1x()
+    project(sv, back)
     for n in range(2):
         rows = pl.ds(n * TILE, TILE)
         dctx[:, rows] = dot_nt(gv[...], wov[back, rows, :]).astype(BF16)
@@ -360,6 +362,7 @@
     attend_back(2)
     attend_back(3)
     dkvb[...] = dkv[...].astype(BF16)
+    fs2z()
     fs3()
 
     def pull_in(n):
@@ -378,6 +381,7 @@
     bs1x()
     bs2()
     bs2x()
+    bs2z()
     bs3()
     fg1()
     bs4()

time: 140 us -> 134 us (0.957)
  Pallas kernels: 135 us -> 128 us
    pallas_call x1, Pallas kernels: 135 us -> 128 us  [local(): pl.pallas_call(kernel, out_shape=(out, out), in_specs=[pl.BlockSpec(memor...]
where the time goes in v4:
time: 134 us; the launch traced here: 132 us
  Pallas kernels  128 us (96%)
  local copies, waits for them, and re-layouts  4.03 us (3%)
    pallas_call x1, Pallas kernels, local(): pl.pallas_call(kernel, out_shape=(out, out), in_specs=[pl.BlockSpec(memor...  128 us
    unnamed x2, local copies, waits for them, and re-layouts  4.03 us

profile of v4, /device:TPU:1, one launch (start us, length us, event | category | flops | bytes accessed | tf_op | source)
XLA Modules:
  0.0 132.5 jit_solution(12191878438161931243)
XLA Ops:
  0.6 127.8 %relay_slot.1 = (bf16[512,4096]{1,0:T(8,128)(2,1)S(1)}, bf16[512,4096]{1,0:T(8,128)(2,1)S(1)}) custom-call(s32[2]{0:T(128)} %bitcast.23, s32[1,4096]{1,0:T(1,128)} %bitcast.22, f32[2,4096]{1,0:T(2,128)} %bitcast.21, bf16[512,4096]{1,0:T(8,128)(2,1)} %bitcast.16, bf16[512,4096]{1,0:T(8,128)(2,1)} %bitcast.17, bf16[512,4096]{1,0:T(8,128)(2,1)} %bitcast.18, ...), custom_call_target="tpu_custom_call" | custom-call | flops 16000000000 | bytes 45000000 | tf_op jit(solution)/shard_map/relay_slot/pallas_call | solution.py:418
  128.4 2.0 %copy.14 = bf16[1,512,4096]{2,1,0:T(8,128)(2,1)} copy(bf16[1,512,4096]{2,1,0:T(8,128)(2,1)S(1)} %bitcast.13) | data formatting | bytes 8388608
  130.4 2.0 %copy.15 = bf16[1,512,4096]{2,1,0:T(8,128)(2,1)} copy(bf16[1,512,4096]{2,1,0:T(8,128)(2,1)S(1)} %bitcast.12) | data formatting | bytes 8388608
